TPU v7x, 32 devices: a whole 2x2x4 slice. The times are simulated.
32 devices in a mesh: pair: 8 (over z, x), aux: 4 (over y, core).
Axes of the slice: x: 2, y: 2, z: 4, core: 2. Of those that a mesh axis runs over, the one named last changes fastest.
Arguments:
- amps: bfloat16 [256, 128, 128], P(('pair', 'aux')), may hold values from -6 to 6
- rotation: bfloat16 [256, 128, 128], P(('pair', 'aux')), may hold values from -0.5 to 0.5
- intersections: bfloat16 [256, 4, 128, 128], P(('pair', 'aux')), may hold values from -0.5 to 0.5
- energies: float32 [256, 128], P(('pair', 'aux')), may hold values from 0.25 to 2
- domains: int32 [256, 2], P(('pair', 'aux')), may hold values from 0 to 7
- owners: int32 [256, 4], P(('pair', 'aux')), may hold values from 0 to 7, all different within a row; in each aligned block of 8 rows (0 to 7, 8 to 15, ...) at most 8 rows name the same one
- slots: int32 [256, 4], P(('pair', 'aux')), may hold values from 0 to 7
- tiles: int32 [256], P(('pair', 'aux')), may hold values from 0 to 7
- blocks: bfloat16 [8, 512, 128], P('aux'), may hold values from -3 to 3
- coeffs: bfloat16 [8, 128, 4096], P('pair', None, 'aux'), may hold values from -0.5 to 0.5
Outputs:
- new_amps: bfloat16 [256, 128, 128], P(('pair', 'aux'))
- density: float32 [8, 128, 4096], P('pair', None, 'aux')
Inputs may be any that keep to these rules, and one draw needn't show every extreme that they name: Each row names distinct owners; among the rows of one device no owner is named by more than 8 entries, a bound that some block reaches.
All inputs are finite; a program needn't handle non-finite values.
Results may differ from a plain program's by a relative error of at most 0.014.
Values may be sent and summed in bfloat16 or wider, within the bound.
A program may use at most 64 MiB of HBM per device.

v0:
```python
import functools

import jax
import jax.numpy as jnp
from jax import lax
from jax.experimental import pallas as pl
from jax.experimental.pallas import tpu as pltpu
from jax.sharding import PartitionSpec as P

MESH = pl.DeviceIdType.MESH
F32 = jnp.float32
BF16 = jnp.bfloat16


def mm(a, b, ca=1, cb=0):
    return lax.dot_general(a, b, (((ca,), (cb,)), ((), ())), preferred_element_type=F32)


def loop(lo, hi, body):
    def step(i, carry):
        body(i)
        return carry

    lax.fori_loop(lo, hi, step, 0)


def remote(src, dst, send, recv, **where):
    return pltpu.make_async_remote_copy(
        src_ref=src, dst_ref=dst, send_sem=send, recv_sem=recv, device_id=where, device_id_type=MESH
    )


def kernel(
    n, lines, n_aux, neighbours,
    owners_in, slots_in, domains_in, tiles_in,
    amps_in, rotation_in, inter_in, energies_in, blocks_in,
    new_amps, total,
    owners, slots, domains, tiles, rotation, inter, energies,
    amps_all, blocks_all, push, sending, xrecv, zsend, zrecv, last_send, last_recv,
    base, rcp, own_term, part, part_own, part_send, part_recv, tot_send, tot_recv,
    in_sem, up_send, down_send, ag_recv, up_late, down_late, late_recv, fwd_send, fwd_recv, blk_send, blk_recv,
    rx_send, rx_recv, rz_send, rz_recv, last_sems,
    t_send, t_recv, a_send, a_recv,
):
    resident, width = amps_in.shape[0], amps_in.shape[1]
    owned = blocks_in.shape[0]
    held = part_own.shape[0]
    me = lax.axis_index("pair")
    aux = lax.axis_index("aux")
    row, side = me // 2, me % 2
    mate = row * 2 + 1 - side

    def rows_of(src):
        return amps_all.at[pl.ds(src * resident, resident)]

    staged = [
        pltpu.make_async_copy(src, dst, in_sem.at[i])
        for i, (src, dst) in enumerate([
            (amps_in, rows_of(me)),
            (blocks_in, blocks_all.at[pl.ds(aux * owned, owned)]),
            (inter_in, inter),
            (owners_in, owners),
            (slots_in, slots),
            (domains_in, domains),
            (tiles_in, tiles),
            (energies_in, energies),
            (rotation_in, rotation),
        ])
    ]
    for copy in staged:
        copy.start()

    barrier = pltpu.get_barrier_semaphore()

    def greet_pair(d):
        pl.semaphore_signal(barrier, inc=1, device_id={"pair": (me + d) % n}, device_id_type=MESH)

    def greet_aux(d):
        pl.semaphore_signal(barrier, inc=1, device_id={"aux": (aux + d) % n_aux}, device_id_type=MESH)

    loop(1, n, greet_pair)
    loop(1, n_aux, greet_aux)
    staged[0].wait()
    staged[1].wait()
    pl.semaphore_wait(barrier, n - 1 + n_aux - 1)

    half_slots = resident // 2

    def own_row(h):
        return rows_of(h * 2 + side)

    def half_row(h, column, q):
        return amps_all.at[pl.ds((h * 2 + column) * resident + q * half_slots, half_slots)]

    def up_copy(h):
        return remote(own_row(h), own_row(h), up_send.at[h], ag_recv.at[h], pair=me + 2)

    def down_copy(h):
        return remote(own_row(h), own_row(h), down_send.at[h], ag_recv.at[h], pair=me - 2)

    def up_late_copy(h):
        src = half_row(h, 1 - side, 1)
        return remote(src, src, up_late.at[h], late_recv.at[h], pair=me + 2)

    def down_late_copy(h):
        src = half_row(h, 1 - side, 1)
        return remote(src, src, down_late.at[h], late_recv.at[h], pair=me - 2)

    def late_copy():
        src = half_row(row, side, 1)
        return remote(src, src, fwd_send.at[lines], late_recv.at[row], pair=mate)

    def fwd_copy(h):
        src = half_row(h, side, 0)
        return remote(src, src, fwd_send.at[h], fwd_recv.at[h], pair=mate)

    def line_arrived(h):
        remote(own_row(h), own_row(h), up_send.at[0], ag_recv.at[h], pair=mate).wait_recv()

    def late_arrived(h):
        here = half_row(h, 1 - side, 1)
        remote(here, here, up_late.at[0], late_recv.at[h], pair=mate).wait_recv()

    def fwd_arrived(h):
        here = half_row(h, 1 - side, 0)
        remote(here, here, fwd_send.at[0], fwd_recv.at[h], pair=mate).wait_recv()

    def block_copy(d):
        here = blocks_all.at[pl.ds(aux * owned, owned)]
        return remote(here, here, blk_send.at[d], blk_recv.at[aux], aux=(aux + d) % n_aux)

    late_copy().start()

    @pl.when(row + 1 < lines)
    def _():
        up_copy(row).start()

    @pl.when(row > 0)
    def _():
        down_copy(row).start()

    fwd_copy(row).start()
    loop(1, n_aux, lambda d: block_copy(d).start())

    def late_step(h, up, down):
        late_arrived(h)

        @pl.when(up)
        def _():
            up_late_copy(h).start()

        @pl.when(down)
        def _():
            down_late_copy(h).start()

    def line_step(s):
        @pl.when(row - s >= 0)
        def _():
            line_arrived(row - s)

            @pl.when(row + 1 < lines)
            def _():
                up_copy(row - s).start()

            fwd_copy(row - s).start()

        @pl.when(row + s < lines)
        def _():
            line_arrived(row + s)

            @pl.when(row > 0)
            def _():
                down_copy(row + s).start()

            fwd_copy(row + s).start()

        @pl.when(row - s >= 0)
        def _():
            late_step(row - s, row + 1 < lines, row < 0)

        @pl.when(row + s < lines)
        def _():
            late_step(row + s, row < 0, row > 0)

    def clear(h):
        for k in range(3):
            zrecv[k, h] = jnp.zeros(zrecv.shape[2:], BF16)

    @pl.when(row == 0)
    def _():
        loop(0, lines, clear)

    @pl.when(row == lines - 1)
    def _():
        loop(0, lines - 1, clear)
        clear(lines)

    for copy in staged[2:]:
        copy.wait()

    group = 4 if resident % 4 == 0 else 1
    some = range(group)

    def push_pairs(i):
        for p in (2 * i, 2 * i + 1):
            own = amps_all[me * resident + p]
            over = [inter[p * neighbours + k] for k in range(neighbours)]
            half = [mm(x, own, 0, 0).astype(BF16) for x in over]
            for k in range(neighbours):
                push[p * neighbours + k] = mm(half[k], over[k]).astype(BF16)

    loop(0, resident // 2, push_pairs)

    chunk = 16

    def gathered(owner, part_at, emit):
        entry, slot = [], []
        for p in range(resident):
            e, s = p * neighbours, jnp.int32(-1)
            for k in range(neighbours):
                hit = owners[k, p] == owner
                e = jnp.where(hit, p * neighbours + k, e)
                s = jnp.where(hit, slots[k, p], s)
            entry.append(e)
            slot.append(s)
        weight = [
            [jnp.where(slot[p] == part_at * half_slots + j, 1.0, 0.0).astype(F32) for p in range(resident)]
            for j in range(half_slots)
        ]

        def rows(c):
            at = pl.ds(pl.multiple_of(c * chunk, chunk), chunk)
            found = [push[entry[p], at, :].astype(F32) for p in range(resident)]
            for j in range(half_slots):
                total = weight[j][0] * found[0]
                for p in range(1, resident):
                    total = total + weight[j][p] * found[p]
                emit(j, at, total)

        loop(0, width // chunk, rows)

    def x_copy(h):
        return remote(sending.at[h], xrecv.at[h], rx_send.at[h], rx_recv.at[h], pair=mate)

    def x_send(i):
        h = (row + jnp.where(2 * row < lines, 2 * lines - i, i)) % lines

        def emit(j, at, total):
            sending[h, j, at, :] = total.astype(BF16)

        gathered(h * 2 + 1 - side, 0, emit)
        x_copy(h).start()

    def z_copy(k, h, up):
        slot = h if up else jnp.where(h == row - 1, lines, h)
        return remote(
            zsend.at[k, h], zrecv.at[k, slot], rz_send.at[k, h], rz_recv.at[k, slot], pair=me + 2 if up else me - 2
        )

    def z_arrived(k, slot):
        here = zrecv.at[k, slot]
        remote(here, here, rz_send.at[k, 0], rz_recv.at[k, slot], pair=mate).wait_recv()

    def z_send(k, early, h, inner, up):
        @pl.when(inner)
        def _():
            z_arrived(k, h)

        if early:
            x_copy(h).wait_recv()

        def emit(j, at, total):
            total = total + zrecv[k, h, j, at, :].astype(F32)
            if early:
                total = total + xrecv[h, j, at, :].astype(F32)
            zsend[k, h, j, at, :] = total.astype(BF16)

        gathered(h * 2 + side if early else h * 2 + (side + k - 1) % 2, 0 if early else 1, emit)
        z_copy(k, h, up).start()

    def z_step(k, early, s, ends):
        @pl.when((row < s) & ((row == 0) == ends))
        def _():
            z_send(k, early, lines - s + row, row > 0, True)

        @pl.when((lines - 1 - row < s) & ((row == lines - 1) == ends))
        def _():
            z_send(k, early, s - lines + row, row < lines - 1, False)

    def z_last(k):
        @pl.when(row > 0)
        def _():
            z_arrived(k, row)

        @pl.when(row < lines - 1)
        def _():
            z_arrived(k, lines)

    def z_both(k, j, at):
        return zrecv[k, row, j, at, :].astype(F32) + zrecv[k, lines, j, at, :].astype(F32)

    def block_arrived(d):
        src = (aux + d) % n_aux
        here = blocks_all.at[pl.ds(src * owned, owned)]
        remote(here, here, blk_send.at[0], blk_recv.at[src], aux=src).wait_recv()

    def integral(i):
        pairs = [i * group + g for g in some]
        rot = [rotation[p] for p in pairs]
        gram = [mm(blocks_all[domains[0, p]], blocks_all[domains[1, p]], 0, 0).astype(BF16) for p in pairs]
        right = [mm(gram[g], rot[g]).astype(BF16) for g in some]
        for p, r, x in zip(pairs, rot, right):
            base[p] = mm(r, x, 0, 0)
            level = jnp.broadcast_to(energies[pl.ds(p, 1), :], (width, width))
            denom = level + level.T
            own = amps_all[me * resident + p].astype(F32)
            inverse = 1.0 / (denom + 1.0)
            rcp[p] = inverse
            own_term[p] = own - denom * own * inverse

    late_step(row, row + 1 < lines, row > 0)
    x_send(1)
    loop(1, lines, lambda s: loop(1, 3, lambda k: z_step(k, False, s, True)))
    loop(2, lines + 1, x_send)
    groups = resident // group

    def step(s):
        line_step(s)
        loop(1, 3, lambda k: z_step(k, False, s, False))
        z_step(0, True, s, True)

        @pl.when(s == 1)
        def _():
            loop(1, n_aux, block_arrived)

        @pl.when(s <= groups)
        def _():
            integral(s - 1)

    loop(1, lines, step)
    loop(lines - 1, groups, integral)

    z_last(2)
    last_copy = remote(last_send, last_recv, last_sems.at[0], last_sems.at[1], pair=mate)

    def emit_mate(j, at, total):
        last_send[j, at, :] = (total + z_both(2, j, at)).astype(BF16)

    gathered(mate, 1, emit_mate)
    last_copy.start()

    loop(0, lines, fwd_arrived)

    def pull_pairs(i):
        for p in (2 * i, 2 * i + 1):
            over = [inter[p * neighbours + k] for k in range(neighbours)]
            half = [
                mm(over[k], amps_all[owners[k, p] * resident + slots[k, p]]).astype(BF16) for k in range(neighbours)
            ]
            total = base[p]
            for k in range(neighbours):
                total = total - mm(half[k], over[k], 1, 1)
            base[p] = own_term[p] - total * rcp[p]

    def pull_step(s):
        z_step(0, True, s, False)

        @pl.when(s - 2 < resident // 2)
        def _():
            pull_pairs(s - 2)

    loop(2, lines, pull_step)
    loop(lines - 2, resident // 2, pull_pairs)

    def own_late(j, at, total):
        p = half_slots + j
        base[p, at, :] += total * rcp[p, at, :]

    def own_early(j, at, total):
        base[j, at, :] += total * rcp[j, at, :]

    gathered(me, 1, own_late)
    gathered(me, 0, own_early)

    def finish(q, k, other):
        pairs = [q * half_slots + g for g in range(half_slots)]
        fresh = []
        for j, p in enumerate(pairs):
            outside = zrecv[k, row, j].astype(F32) + zrecv[k, lines, j].astype(F32) + other[j].astype(F32)
            fresh.append((base[p] + outside * rcp[p]).astype(BF16))
        for p, x in zip(pairs, fresh):
            new_amps[p] = x
        rot = [rotation[p] for p in pairs]
        pair_density = [(mm(x, x, 1, 1) * (1.0 / width)).astype(BF16) for x in fresh]
        rotated = [mm(r, x).astype(BF16) for r, x in zip(rot, pair_density)]
        for p, r, x in zip(pairs, rot, rotated):
            part[p] = mm(x, r, 1, 1)

    z_last(1)
    last_copy.wait_recv()
    finish(1, 1, last_recv)
    z_last(0)
    x_copy(row).wait_recv()
    finish(0, 0, xrecv.at[row])

    def t_copy(d):
        t = (me + d) % n
        return remote(part_send.at[t], part_recv.at[me], t_send.at[d], t_recv.at[me], pair=t)

    def tile_part(t, j):
        total = jnp.where(tiles[0] == t * held + j, 1.0, 0.0).astype(F32) * part[0]
        for p in range(1, resident):
            total = total + jnp.where(tiles[p] == t * held + j, 1.0, 0.0).astype(F32) * part[p]
        return total

    def tile_send(d):
        t = (me + d) % n
        for j in range(held):
            part_send[t, j] = tile_part(t, j).astype(BF16)
        t_copy(d).start()

    loop(1, n, tile_send)
    for j in range(held):
        part_own[j] = tile_part(me, j)

    def tile_add(d):
        src = (me + d) % n
        here = part_recv.at[src]
        remote(here, here, t_send.at[0], t_recv.at[src], pair=src).wait_recv()
        for j in range(held):
            part_own[j] += part_recv[src, j].astype(F32)

    loop(1, n, tile_add)
    tot_send[...] = part_own[...].astype(BF16)

    def a_copy(d):
        return remote(tot_send, tot_recv.at[aux], a_send.at[d], a_recv.at[aux], aux=(aux + d) % n_aux)

    loop(1, n_aux, lambda d: a_copy(d).start())

    def tot_add(d):
        src = (aux + d) % n_aux
        here = tot_recv.at[src]
        remote(here, here, a_send.at[0], a_recv.at[src], aux=src).wait_recv()
        for j in range(held):
            part_own[j] += tot_recv[src, j].astype(F32)

    loop(1, n_aux, tot_add)
    for j in range(held):
        total[j] = part_own[j]

    def line_left(h):
        @pl.when((row + 1 < lines) & (h <= row))
        def _():
            up_copy(h).wait_send()
            up_late_copy(h).wait_send()

        @pl.when((row > 0) & (h >= row))
        def _():
            down_copy(h).wait_send()
            down_late_copy(h).wait_send()

        fwd_copy(h).wait_send()
        x_copy(h).wait_send()

        @pl.when(h > row)
        def _():
            for k in range(3):
                z_copy(k, h, True).wait_send()

        @pl.when(h < row)
        def _():
            for k in range(3):
                z_copy(k, h, False).wait_send()

    loop(0, lines, line_left)
    late_copy().wait_send()
    last_copy.wait_send()
    loop(1, n_aux, lambda d: block_copy(d).wait_send())
    loop(1, n, lambda d: t_copy(d).wait_send())
    loop(1, n_aux, lambda d: a_copy(d).wait_send())


def finishing(factor, fresh, total_in, coeffs_in, new_amps, density, coeffs, total, result, sems):
    load = pltpu.make_async_copy(coeffs_in, coeffs, sems.at[0])
    load.start()
    sums = pltpu.make_async_copy(total_in, total, sems.at[2])
    sums.start()
    keep = pltpu.make_async_copy(fresh, new_amps, sems.at[1])
    keep.start()
    sums.wait()
    load.wait()
    held = coeffs.shape[0]
    stores = [pltpu.make_async_copy(result.at[j], density.at[j], sems.at[3 + j]) for j in range(held)]
    for j in range(held):
        high = total[j].astype(BF16)
        low = (total[j] - high.astype(F32)).astype(BF16)
        result[j] = (mm(high, coeffs[j]) + mm(low, coeffs[j])) * factor
        stores[j].start()
    for store in stores:
        store.wait()
    keep.wait()


def local(n, n_aux, amps, rotation, intersections, energies, domains, owners, slots, tiles, blocks, coeffs):
    resident, width = amps.shape[0], amps.shape[1]
    neighbours = owners.shape[1]
    entries = resident * neighbours
    lines = n // 2
    held = coeffs.shape[0]
    square = (width, width)
    dma = pltpu.SemaphoreType.DMA
    scratch = [
        (rotation.shape, BF16),
        ((entries,) + square, BF16),
        (energies.shape, F32),
        ((n * resident,) + square, BF16),
        ((n_aux * blocks.shape[0],) + blocks.shape[1:], BF16),
        ((entries,) + square, BF16),
        ((lines, resident // 2) + square, BF16),
        ((lines, resident // 2) + square, BF16),
        ((3, lines, resident // 2) + square, BF16),
        ((3, lines + 1, resident // 2) + square, BF16),
        ((resident // 2,) + square, BF16),
        ((resident // 2,) + square, BF16),
        ((resident,) + square, F32),
        ((resident,) + square, F32),
        ((resident,) + square, F32),
        ((resident,) + square, F32),
        ((held,) + square, F32),
        ((n, held) + square, BF16),
        ((n, held) + square, BF16),
        ((held,) + square, BF16),
        ((n_aux, held) + square, BF16),
    ]
    sems = [9] + [lines] * 6 + [lines + 1, lines, n_aux, n_aux, lines, lines, (3, lines), (3, lines + 1), 2]
    sems += [n, n, n_aux, n_aux]
    hbm = pl.BlockSpec(memory_space=pltpu.HBM)
    vmem = pl.BlockSpec(memory_space=pltpu.VMEM)
    out_shape = (
        jax.ShapeDtypeStruct(amps.shape, BF16),
        jax.ShapeDtypeStruct((held,) + square, F32),
    )
    fresh, total = pl.pallas_call(
        functools.partial(kernel, n, lines, n_aux, neighbours),
        out_shape=out_shape,
        in_specs=[hbm] * 9,
        out_specs=(vmem, vmem),
        scratch_shapes=[pltpu.SMEM(x.shape, jnp.int32) for x in (owners.T, slots.T, domains.T, tiles)]
        + [pltpu.VMEM(*s) for s in scratch]
        + [dma(k if isinstance(k, tuple) else (k,)) for k in sems],
        compiler_params=pltpu.CompilerParams(
            collective_id=0, has_side_effects=True, vmem_limit_bytes=60 << 20
        ),
    )(
        owners.T,
        slots.T,
        domains.T,
        tiles,
        amps,
        rotation,
        intersections.reshape((entries,) + square),
        energies,
        blocks,
    )
    return pl.pallas_call(
        functools.partial(finishing, 1.0 / (resident * n_aux)),
        out_shape=(
            jax.ShapeDtypeStruct(amps.shape, BF16),
            jax.ShapeDtypeStruct((held, width, coeffs.shape[2]), F32),
        ),
        in_specs=[hbm] * 3,
        out_specs=(hbm, hbm),
        scratch_shapes=[
            pltpu.VMEM(coeffs.shape, BF16),
            pltpu.VMEM((held,) + square, F32),
            pltpu.VMEM((held, width, coeffs.shape[2]), F32),
            dma((3 + held,)),
        ],
        compiler_params=pltpu.CompilerParams(vmem_limit_bytes=60 << 20),
    )(fresh, total, coeffs)


def solution(mesh):
    return jax.shard_map(
        functools.partial(local, mesh.shape["pair"], mesh.shape["aux"]),
        mesh=mesh,
        in_specs=(
            P(("pair", "aux"), None, None),
            P(("pair", "aux"), None, None),
            P(("pair", "aux"), None, None, None),
            P(("pair", "aux"), None),
            P(("pair", "aux"), None),
            P(("pair", "aux"), None),
            P(("pair", "aux"), None),
            P(("pair", "aux")),
            P("aux", None, None),
            P("pair", None, "aux"),
        ),
        out_specs=(P(("pair", "aux"), None, None), P("pair", None, "aux")),
        check_vma=False,
    )
```

profile of v0, /device:TPU:0, one launch (start us, length us, event | category | flops | bytes accessed | tf_op | source)
XLA Modules:
  0.0 68.3 jit_solution(13828267165528646617)
XLA Ops:
  0.6 58.5 %shard_map.113 = (bf16[8,128,128]{2,1,0:T(8,128)(2,1)}, f32[1,128,128]{2,1,0:T(8,128)}) custom-call(s32[4,8]{1,0:T(4,128)} %bitcast.5, s32[4,8]{1,0:T(4,128)} %bitcast.6, s32[2,8]{1,0:T(2,128)} %bitcast.7, s32[8]{0:T(128)} %tiles_in.1, bf16[8,128,128]{2,1,0:T(8,128)(2,1)} %amps_in.1, bf16[8,128,128]{2,1,0:T(8,128)(2,1)} %rotation_in.1, ...), custom_call_target="tpu_custom_call" | custom-call | tf_op jit(solution)/shard_map/pallas_call | solution.py:544
  59.2 9.1 %shard_map.114 = (bf16[8,128,128]{2,1,0:T(8,128)(2,1)}, f32[1,128,1024]{2,1,0:T(8,128)}) custom-call(bf16[8,128,128]{2,1,0:T(8,128)(2,1)} %get-tuple-element.4.fresh, f32[1,128,128]{2,1,0:T(8,128)} %get-tuple-element.5.total_in, bf16[1,128,1024]{2,1,0:T(8,128)(2,1)} %coeffs_in.1), custom_call_target="tpu_custom_call" | custom-call | tf_op jit(solution)/shard_map/pallas_call | solution.py:566
where the time goes:
time: 68.4 us; the launch traced here: 68.3 us
  Pallas kernels  67.6 us (99%)
    pallas_call x1, Pallas kernels, local(): pl.pallas_call(functools.partial(kernel, n, lines, n_aux, neighbours), ou...  58.5 us
    pallas_call x1, Pallas kernels, local(): pl.pallas_call(functools.partial(finishing, 1.0 / (resident * n_aux)), ou...  9.08 us

commit v1 on v0

--- a/solution.py
+++ b/solution.py
@@ -481,17 +481,20 @@
     loop(1, n_aux, lambda d: a_copy(d).wait_send())
 
 
-def finishing(factor, fresh, total_in, coeffs_in, new_amps, density, coeffs, total, result, sems):
+def finishing(factor, fresh, total_in, coeffs_in, new_amps, density, coeffs, total, result, passing, sems):
     load = pltpu.make_async_copy(coeffs_in, coeffs, sems.at[0])
     load.start()
     sums = pltpu.make_async_copy(total_in, total, sems.at[2])
     sums.start()
-    keep = pltpu.make_async_copy(fresh, new_amps, sems.at[1])
+    fetch = pltpu.make_async_copy(fresh, passing, sems.at[1])
+    fetch.start()
+    fetch.wait()
+    keep = pltpu.make_async_copy(passing, new_amps, sems.at[3])
     keep.start()
     sums.wait()
     load.wait()
     held = coeffs.shape[0]
-    stores = [pltpu.make_async_copy(result.at[j], density.at[j], sems.at[3 + j]) for j in range(held)]
+    stores = [pltpu.make_async_copy(result.at[j], density.at[j], sems.at[4 + j]) for j in range(held)]
     for j in range(held):
         high = total[j].astype(BF16)
         low = (total[j] - high.astype(F32)).astype(BF16)
@@ -575,7 +578,8 @@
             pltpu.VMEM(coeffs.shape, BF16),
             pltpu.VMEM((held,) + square, F32),
             pltpu.VMEM((held, width, coeffs.shape[2]), F32),
-            dma((3 + held,)),
+            pltpu.VMEM(amps.shape, BF16),
+            dma((4 + held,)),
         ],
         compiler_params=pltpu.CompilerParams(vmem_limit_bytes=60 << 20),
     )(fresh, total, coeffs)

time: 68.4 us -> 61.5 us (0.90)
  Pallas kernels: 67.6 us -> 60.7 us
    pallas_call x1, Pallas kernels: 9.08 us -> 2.19 us  [local(): pl.pallas_call(functools.partial(finishing, 1.0 / (resident * n_aux)), ou...]
where the time goes in v1:
time: 61.5 us; the launch traced here: 61.4 us
  Pallas kernels  60.7 us (99%)
  between operations  0.64 us (1%)
    pallas_call x1, Pallas kernels, local(): pl.pallas_call(functools.partial(kernel, n, lines, n_aux, neighbours), ou...  58.5 us
    pallas_call x1, Pallas kernels, local(): pl.pallas_call(functools.partial(finishing, 1.0 / (resident * n_aux)), ou...  2.19 us

profile of v1, /device:TPU:0, one launch (start us, length us, event | category | flops | bytes accessed | tf_op | source)
XLA Modules:
  0.0 61.4 jit_solution(7906782672353467996)
XLA Ops:
  0.6 58.5 %shard_map.113 = (bf16[8,128,128]{2,1,0:T(8,128)(2,1)}, f32[1,128,128]{2,1,0:T(8,128)}) custom-call(s32[4,8]{1,0:T(4,128)} %bitcast.5, s32[4,8]{1,0:T(4,128)} %bitcast.6, s32[2,8]{1,0:T(2,128)} %bitcast.7, s32[8]{0:T(128)} %tiles_in.1, bf16[8,128,128]{2,1,0:T(8,128)(2,1)} %amps_in.1, bf16[8,128,128]{2,1,0:T(8,128)(2,1)} %rotation_in.1, ...), custom_call_target="tpu_custom_call" | custom-call | tf_op jit(solution)/shard_map/pallas_call | solution.py:547
  59.2 2.2 %shard_map.114 = (bf16[8,128,128]{2,1,0:T(8,128)(2,1)}, f32[1,128,1024]{2,1,0:T(8,128)}) custom-call(bf16[8,128,128]{2,1,0:T(8,128)(2,1)} %get-tuple-element.4.fresh, f32[1,128,128]{2,1,0:T(8,128)} %get-tuple-element.5.total_in, bf16[1,128,1024]{2,1,0:T(8,128)(2,1)} %coeffs_in.1), custom_call_target="tpu_custom_call" | custom-call | tf_op jit(solution)/shard_map/pallas_call | solution.py:569

commit v2 on v1

--- a/solution.py
+++ b/solution.py
@@ -209,7 +209,9 @@
             for k in range(neighbours):
                 push[p * neighbours + k] = mm(half[k], over[k]).astype(BF16)
 
-    loop(0, resident // 2, push_pairs)
+    loop(0, resident // 4, push_pairs)
+    late_step(row, row + 1 < lines, row > 0)
+    loop(resident // 4, resident // 2, push_pairs)
 
     chunk = 16
 
@@ -318,7 +320,6 @@
             rcp[p] = inverse
             own_term[p] = own - denom * own * inverse
 
-    late_step(row, row + 1 < lines, row > 0)
     x_send(1)
     loop(1, lines, lambda s: loop(1, 3, lambda k: z_step(k, False, s, True)))
     loop(2, lines + 1, x_send)

time: 61.5 us -> 61.5 us (level)
  no operation moved by 1% of the time
where the time goes in v2:
time: 61.5 us; the launch traced here: 61.4 us
  Pallas kernels  60.7 us (99%)
  between operations  0.64 us (1%)
    pallas_call x1, Pallas kernels, local(): pl.pallas_call(functools.partial(kernel, n, lines, n_aux, neighbours), ou...  58.5 us
    pallas_call x1, Pallas kernels, local(): pl.pallas_call(functools.partial(finishing, 1.0 / (resident * n_aux)), ou...  2.19 us

profile of v2, /device:TPU:0, one launch (start us, length us, event | category | flops | bytes accessed | tf_op | source)
XLA Modules:
  0.0 61.4 jit_solution(15473450911059559971)
XLA Ops:
  0.6 58.5 %shard_map.113 = (bf16[8,128,128]{2,1,0:T(8,128)(2,1)}, f32[1,128,128]{2,1,0:T(8,128)}) custom-call(s32[4,8]{1,0:T(4,128)} %bitcast.5, s32[4,8]{1,0:T(4,128)} %bitcast.6, s32[2,8]{1,0:T(2,128)} %bitcast.7, s32[8]{0:T(128)} %tiles_in.1, bf16[8,128,128]{2,1,0:T(8,128)(2,1)} %amps_in.1, bf16[8,128,128]{2,1,0:T(8,128)(2,1)} %rotation_in.1, ...), custom_call_target="tpu_custom_call" | custom-call | tf_op jit(solution)/shard_map/pallas_call | solution.py:548
  59.2 2.2 %shard_map.114 = (bf16[8,128,128]{2,1,0:T(8,128)(2,1)}, f32[1,128,1024]{2,1,0:T(8,128)}) custom-call(bf16[8,128,128]{2,1,0:T(8,128)(2,1)} %get-tuple-element.4.fresh, f32[1,128,128]{2,1,0:T(8,128)} %get-tuple-element.5.total_in, bf16[1,128,1024]{2,1,0:T(8,128)(2,1)} %coeffs_in.1), custom_call_target="tpu_custom_call" | custom-call | tf_op jit(solution)/shard_map/pallas_call | solution.py:570
